TPU v7x, 32 devices: a whole 2x2x4 slice. The times are simulated.
32 devices in a mesh: section: 2 (over x), cp: 4 (over y, core), tp: 4 (over z).
Axes of the slice: x: 2, y: 2, z: 4, core: 2. Of those that a mesh axis runs over, the one named last changes fastest.
Arguments:
- rollout_rows: bfloat16 [512, 8192], P(('section', 'cp'), 'tp'), may hold values from -60 to 60
- lengths: int32 [2], replicated, may hold values from 1 to 384, 512 in all
- block_owner: int32 [8], replicated, may hold values from 0 to 7, each once
- norm_gain: float32 [2, 8192], P('section', 'tp'), may hold values from 0.1 to 1.9
- w_qkv: bfloat16 [2, 3, 8192, 8192], P('section', None, 'tp', 'cp'), may hold values from -1 to 1
- w_out: bfloat16 [2, 8192, 8192], P('section', 'cp', 'tp'), may hold values from -0.5 to 0.5
Outputs:
- scored: bfloat16 [2, 512, 8192], P(None, ('section', 'cp'), 'tp')
Inputs may be any that keep to these rules, and one draw needn't show every extreme that they name: The 2 lengths sum to 512; neither is over 384. `block_owner`: every owner block appears once.
All inputs are finite; a program needn't handle non-finite values.
Results may differ from a plain program's by a relative error of at most 0.022.
Values may be sent and summed in bfloat16 or wider, within the bound.
A program may use at most 128 MiB of HBM per device.

v0:
```python
import math

import jax
import jax.numpy as jnp
from jax import lax
from jax.sharding import PartitionSpec as P

D = 8192
HEAD = 128


def layout_position(layout_rows, tokens, tp_count):
    quarter = tokens // tp_count
    halfblock = quarter // 2
    owner_index = layout_rows // quarter
    second = layout_rows % quarter // halfblock
    offset = layout_rows % halfblock
    block_index = 2 * owner_index + second
    return block_index * halfblock + offset


def layout_row(position, tokens, tp_count):
    quarter = tokens // tp_count
    halfblock = quarter // 2
    block_index = position // halfblock
    offset = position % halfblock
    second = block_index % 2
    owner_index = block_index // 2
    return owner_index * quarter + second * halfblock + offset


def on_device(rollout_rows, lengths, block_owner, norm_gain, w_qkv, w_out):
    tp_count = lax.axis_size("tp")
    cp_count = lax.axis_size("cp")
    sections = lax.axis_size("section")
    own_rows, width_here = rollout_rows.shape
    blocks = sections * cp_count
    tokens = own_rows * blocks
    actor_rows = lax.all_gather(rollout_rows, ("section", "cp"), axis=0, tiled=True)
    layout_rows = jnp.arange(tokens, dtype=jnp.int32)
    position = layout_position(layout_rows, tokens, tp_count)
    source = block_owner[position // own_rows] * own_rows + position % own_rows
    rows_in = jnp.take(actor_rows, source, axis=0)
    seq_ends = jnp.cumsum(lengths)
    sequence = jnp.sum((position[:, None] >= seq_ends[None, :]).astype(jnp.int32), axis=1)
    squares = jnp.sum(jnp.square(rows_in.astype(jnp.float32)), axis=1)
    total_squares = lax.psum(squares, "tp")
    inverse_rms = lax.rsqrt(total_squares / D + 1e-05)
    normed = (rows_in.astype(jnp.float32) * norm_gain[0][None, :] * inverse_rms[:, None]).astype(
        jnp.bfloat16
    )
    qkv_weights = w_qkv[0]
    local_rows = tokens // tp_count
    halfblock = local_rows // 2
    heads_here = qkv_weights.shape[2] // HEAD
    first_local = lax.axis_index("tp") * local_rows
    query_pos = lax.dynamic_slice_in_dim(position, first_local, local_rows, 0).reshape(2, halfblock)
    query_seq = lax.dynamic_slice_in_dim(sequence, first_local, local_rows, 0).reshape(2, halfblock)
    inv_sqrt = 1.0 / math.sqrt(HEAD)
    initial = (
        jnp.full((2, heads_here, halfblock), -1e30, jnp.float32),
        jnp.zeros((2, heads_here, halfblock), jnp.float32),
        jnp.zeros((2, heads_here, halfblock, HEAD), jnp.float32),
    )
    projected = lax.psum_scatter(
        jnp.einsum("rd,kdc->rkc", normed, qkv_weights, preferred_element_type=jnp.float32),
        "tp",
        scatter_dimension=0,
        tiled=True,
    ).astype(jnp.bfloat16)
    query_blocks = projected[:, 0].reshape(2, halfblock, heads_here, HEAD)
    key_part = lax.all_gather(projected[:, 1], "tp", axis=0, tiled=True)
    value_part = lax.all_gather(projected[:, 2], "tp", axis=0, tiled=True)
    key_count = key_part.shape[0]
    key_heads = key_part.reshape(key_count, heads_here, HEAD)
    value_heads = value_part.reshape(key_count, heads_here, HEAD)
    results = []
    for sub_block in range(2):
        allowed = (query_seq[sub_block][:, None] == sequence[None, :]) & (
            position[None, :] <= query_pos[sub_block][:, None]
        )
        query_block = query_blocks[sub_block]

        def update(state_now):
            row_peak, row_total, weighted = state_now
            scores = (
                jnp.einsum(
                    "qhd,khd->hqk", query_block, key_heads, preferred_element_type=jnp.float32
                )
                * inv_sqrt
            )
            scores = jnp.where(allowed[None], scores, -1e30)
            new_peak = jnp.maximum(row_peak, jnp.max(scores, axis=2))
            weights_now = jnp.where(allowed[None], jnp.exp(scores - new_peak[:, :, None]), 0.0)
            row_total = jnp.sum(weights_now, axis=2)
            probabilities = weights_now.astype(jnp.bfloat16)
            weighted = jnp.einsum(
                "hqk,khd->hqd", probabilities, value_heads, preferred_element_type=jnp.float32
            )
            return (new_peak, row_total, weighted)

        def unchanged(state_now):
            return state_now

        results.append(
            lax.cond(
                jnp.any(allowed),
                update,
                unchanged,
                (initial[0][sub_block], initial[1][sub_block], initial[2][sub_block]),
            )
        )
    attended = (
        jnp.stack([results[0][2], results[1][2]])
        / jnp.stack([results[0][1], results[1][1]])[:, :, :, None]
    )
    attended = (
        attended.transpose(0, 2, 1, 3).reshape(local_rows, heads_here * HEAD).astype(jnp.bfloat16)
    )
    gathered = lax.all_gather(attended, "tp", axis=0, tiled=True)
    group_rows = sections * own_rows
    target_rows = jnp.arange(tokens, dtype=jnp.int32)
    cp_index = target_rows // group_rows
    owner_section = target_rows % group_rows // own_rows
    inner = target_rows % own_rows
    actor_block = owner_section * cp_count + cp_index
    block_ids = jnp.arange(blocks, dtype=jnp.int32)
    inverse_owner = jnp.sum(
        jnp.where(block_owner[None, :] == block_ids[:, None], block_ids[None, :], 0), axis=1
    )
    packed_pos = inverse_owner[actor_block] * own_rows + inner
    ordered = jnp.take(gathered, layout_row(packed_pos, tokens, tp_count), axis=0)
    out_weight = w_out[0]
    summed = lax.psum_scatter(
        jnp.dot(ordered, out_weight, preferred_element_type=jnp.float32).astype(jnp.bfloat16),
        "cp",
        scatter_dimension=0,
        tiled=True,
    )
    branch = summed.reshape(sections, own_rows, width_here)
    return lax.all_to_all(branch, "section", split_axis=0, concat_axis=0, tiled=True)


def solution(mesh):
    return jax.shard_map(
        on_device,
        mesh=mesh,
        in_specs=(
            P(("section", "cp"), "tp"),
            P(),
            P(),
            P("section", "tp"),
            P("section", None, "tp", "cp"),
            P("section", "cp", "tp"),
        ),
        out_specs=P(None, ("section", "cp"), "tp"),
        check_vma=False,
    )
```

profile of v0, /device:TPU:0, one launch (start us, length us, event | category | flops | bytes accessed | tf_op | source)
XLA Modules:
  0.0 515.5 jit_solution(6560948798802980872)
XLA Ops:
  6.5 0.7 all-gather.7.cloned.1.call-update
  7.4 1.6 fusion.97
  8.9 4.2 compare_select_fusion.8
  13.9 26.0 %all-gather.7.cloned.1.call-done = bf16[512,2048]{1,0:T(8,128)(2,1)} async-done(((bf16[64,2048]{1,0:T(8,128)(2,1)}), bf16[512,2048]{1,0:T(8,128)(2,1)}) %all-gather.7.cloned.1.call-update) | async-done | bytes 2097168 | tf_op jit(solution)/shard_map/all_gather | solution.py:39
  39.9 6.3 %gather_fusion = bf16[512,2048]{1,0:T(8,128)(2,1)S(1)} fusion(bf16[512,2048]{1,0:T(8,128)(2,1)} %all-gather.7.cloned.1.call-done, s32[1024]{0:T(1024)S(1)} %pad_clamp_fusion.1), kind=kCustom, calls=%fused_computation.clone | custom fusion | bytes 4196352 | tf_op jit(solution)/shard_map/jit(_take)/gather | solution.py:43
  46.9 11.7 %psum.7 = f32[512]{0:T(512)S(1)} all-reduce(f32[512]{0:T(512)S(1)} %fusion.46), channel_id=1, replica_groups=mesh['section'=2,'cp'=4,'tp'=4] {'tp'}, use_global_device_ids=true, to_apply=%region_4.6 | all-reduce | flops 512 | bytes 4096 | tf_op jit(solution)/shard_map/psum | solution.py:47
  58.6 21.8 %fusion.40 = f32[512,3,2048]{2,0,1:T(8,128)} fusion(bf16[1,3,2048,2048]{3,2,1,0:T(8,128)(2,1)} %param.16, f32[512]{0:T(512)S(1)} %add_rsqrt_fusion, f32[2048]{0:T(1024)S(1)} %bitcast.78, bf16[512,2048]{1,0:T(8,128)(2,1)S(1)} %gather_fusion, pred[512]{0:T(512)(128)(4,1)S(1)} %get-tuple-element.74), kind=kOutput, calls=%fused_computation.44 | convolution fusion | flops 12890144768 | bytes 39856640 | tf_op jit(solution)/shard_map/rd,kdc->rkc/dot_general | solution.py:66
  80.4 209.2 %reduce-scatter.3.cloned.1.call-done = f32[128,3,2048]{2,0,1:T(8,128)} async-done(((f32[512,3,2048]{2,0,1:T(8,128)}), f32[128,3,2048]{2,0,1:T(8,128)}) %reduce-scatter.3.cloned.1.call-update) | async-done | bytes 3145744 | tf_op jit(solution)/shard_map/reduce_scatter | solution.py:65
  289.6 2.1 convert_element_type.41
  291.8 1.2 copy-done
  292.9 1.1 fusion.93
  295.1 0.8 fusion.91
  297.2 44.0 %all-gather.11.cloned.1.call-done = bf16[512,1,2048]{2,0,1:T(8,128)(2,1)} async-done(((bf16[128,1,2048]{2,0,1:T(8,128)(2,1)}), bf16[512,1,2048]{2,0,1:T(8,128)(2,1)}) %all-gather.11.cloned.1.call-update) | async-done | bytes 2097168 | tf_op jit(solution)/shard_map/all_gather | solution.py:72
  341.1 2.2 copy.30
  343.3 43.9 %all-gather.13.cloned.1.call-done = bf16[512,1,2048]{2,0,1:T(8,128)(2,1)} async-done(((bf16[128,1,2048]{2,0,1:T(8,128)(2,1)}), bf16[512,1,2048]{2,0,1:T(8,128)(2,1)}) %all-gather.13.cloned.1.call-update) | async-done | bytes 2097168 | tf_op jit(solution)/shard_map/all_gather | solution.py:73
  387.2 3.5 copy.31
  390.8 6.4 %conditional.2 = (f32[1,16,64]{2,1,0:T(8,128)S(1)}, f32[1,16,64,128]{3,2,1,0:T(8,128)S(1)}) conditional(s32[]{:T(128)} %convert_element_type.38, () %tuple.30, (pred[64,512]{1,0:T(8,128)(4,1)S(1)}, bf16[128,3,2048]{2,0,1:T(8,128)(2,1)}, bf16[512,16,128]{2,1,0:T(8,128)(2,1)S(1)}, bf16[512,16,128]{2,1,0:T(8,128)(2,1)}) %tuple.85), branch_computations={%region_6.8_spmd, %region_7.11_spmd} | conditional | flops 275250176 | bytes 12443664 | solution.py:106
  390.8 1.0 slice_bitcast_fusion
  391.8 1.5 fusion.4
  393.3 3.2 fusion.7
  397.2 6.4 %conditional.3 = (f32[1,16,64]{2,1,0:T(8,128)S(1)}, f32[1,16,64,128]{3,2,1,0:T(8,128)S(1)}) conditional(s32[]{:T(128)} %convert_element_type.42, () %tuple.32, (pred[64,512]{1,0:T(8,128)(4,1)S(1)}, bf16[128,3,2048]{2,0,1:T(8,128)(2,1)}, bf16[512,16,128]{2,1,0:T(8,128)(2,1)S(1)}, bf16[512,16,128]{2,1,0:T(8,128)(2,1)}) %tuple.86), branch_computations={%region_11.13_spmd, %region_12.16_spmd} | conditional | flops 275250176 | bytes 12443664 | solution.py:106
  397.2 1.0 slice_bitcast_fusion.1
  398.2 1.5 fusion.24
  399.7 3.2 fusion.27
  404.3 0.9 copy.58
  406.4 4.3 compare_select_fusion.2
  411.3 38.8 %all-gather.9.cloned.1.call-done = bf16[512,2048]{1,0:T(8,128)(2,1)} async-done(((bf16[128,2048]{1,0:T(8,128)(2,1)}), bf16[512,2048]{1,0:T(8,128)(2,1)}) %all-gather.9.cloned.1.call-update) | async-done | bytes 2097168 | tf_op jit(solution)/shard_map/all_gather | solution.py:120
  450.1 6.3 %gather_fusion.1 = bf16[512,2048]{1,0:T(8,128)(2,1)S(1)} fusion(bf16[512,2048]{1,0:T(8,128)(2,1)} %all-gather.9.cloned.1.call-done, s32[1024]{0:T(1024)S(1)} %pad_clamp_fusion), kind=kCustom, calls=%fused_computation.1.clone | custom fusion | bytes 4196352 | tf_op jit(solution)/shard_map/jit(_take)/gather | solution.py:132
  456.4 9.4 %fusion.47 = bf16[512,2048]{1,0:T(8,128)(2,1)} fusion(bf16[1,2048,2048]{2,1,0:T(8,128)(2,1)} %param.17, bf16[512,2048]{1,0:T(8,128)(2,1)S(1)} %gather_fusion.1, pred[512]{0:T(512)(128)(4,1)S(1)} %get-tuple-element.70), kind=kOutput, calls=%fused_computation.53 | convolution fusion | flops 4297064448 | bytes 12583424 | tf_op jit(solution)/shard_map/dot_general | solution.py:135
  465.8 30.3 %reduce-scatter.5.cloned.1.call-done = bf16[128,2048]{1,0:T(8,128)(2,1)} async-done(((bf16[512,2048]{1,0:T(8,128)(2,1)}), bf16[128,2048]{1,0:T(8,128)(2,1)}) %reduce-scatter.5.cloned.1.call-update) | async-done | bytes 524304 | tf_op jit(solution)/shard_map/reduce_scatter | solution.py:134
  496.1 11.7 %all_to_all.5 = bf16[2,64,2048]{2,1,0:T(8,128)(2,1)S(1)} all-to-all(bf16[2,64,2048]{2,1,0:T(8,128)(2,1)} %bitcast.72), channel_id=1, replica_groups=mesh['section'=2,'cp'=4,'tp'=4] {'section'}, dimensions={0} | all-to-all | bytes 1048576 | tf_op jit(solution)/shard_map/all_to_all | solution.py:141
  507.8 0.8 copy.68
  (43 shorter events, 6.6 us)
Async XLA Ops:
  6.5 33.3 %all-gather.7.cloned.1.call-start = ((), (), s32[]{:S(2)}) async-start(), calls=%async_computation.3 | async-start | bytes 2359296 | tf_op jit(solution)/shard_map/all_gather | solution.py:39
  7.3 282.4 %reduce-scatter.3.cloned.1.call-start = ((), (), s32[]{:S(2)}) async-start(), calls=%async_computation.4 | async-start | bytes 15728640 | tf_op jit(solution)/shard_map/reduce_scatter | solution.py:65
  46.1 12.4 %copy-start.2 = (f32[1,2048]{1,0:T(1,128)S(1)}, f32[1,2048]{1,0:T(1,128)}, u32[]{:S(2)}) copy-start(f32[1,2048]{1,0:T(1,128)} %param.15) | copy-start | bytes 24580
  80.4 260.8 %all-gather.11.cloned.1.call-start = ((), (), s32[]{:S(2)}) async-start(), calls=%async_computation.7 | async-start | bytes 2621440 | tf_op jit(solution)/shard_map/all_gather | solution.py:72
  291.7 1.2 copy-start
  292.9 1.7 copy-start.3
  294.0 93.2 %all-gather.13.cloned.1.call-start = ((), (), s32[]{:S(2)}) async-start(), calls=%async_computation.8 | async-start | bytes 2621440 | tf_op jit(solution)/shard_map/all_gather | solution.py:73
  294.6 155.5 %all-gather.9.cloned.1.call-start = ((), (), s32[]{:S(2)}) async-start(), calls=%async_computation.5 | async-start | bytes 2621440 | tf_op jit(solution)/shard_map/all_gather | solution.py:120
  403.6 2.0 copy-start.1
  405.3 90.8 %reduce-scatter.5.cloned.1.call-start = ((), (), s32[]{:S(2)}) async-start(), calls=%async_computation.6 | async-start | bytes 2621440 | tf_op jit(solution)/shard_map/reduce_scatter | solution.py:134
Sparse Core Ops, SparseCore 0:
  9.2 30.5 all-gather.6
  80.5 209.0 reduce-scatter.2
  294.1 46.9 all-gather.10
  342.6 44.6 all-gather.12
  405.4 44.6 all-gather.8
  465.9 30.1 reduce-scatter.4
where the time goes:
time: 516 us; the launch traced here: 515 us
  waiting for transfers between devices  393 us (76%)
  matrix products  40.6 us (8%)
  local copies, waits for them, and re-layouts  27.1 us (5%)
  blocking collectives  23.4 us (5%)
  other arithmetic  15.7 us (3%)
  between operations  14.8 us (3%)
    reduce_scatter x1, waiting for transfers between devices, on_device(): lax.psum_scatter(jnp.einsum('rd,kdc->rkc', normed, qkv_weights, preferred...  209 us
    all_gather x1, waiting for transfers between devices, on_device(): key_part = lax.all_gather(projected[:, 1], 'tp', axis=0, tiled=True)  44 us
    all_gather x1, waiting for transfers between devices, on_device(): value_part = lax.all_gather(projected[:, 2], 'tp', axis=0, tiled=True)  43.9 us
    all_gather x1, waiting for transfers between devices, on_device(): gathered = lax.all_gather(attended, 'tp', axis=0, tiled=True)  38.8 us
    reduce_scatter x1, waiting for transfers between devices, on_device(): lax.psum_scatter(jnp.dot(ordered, out_weight, preferred_element_type=jnp....  30.3 us
    all_gather x1, waiting for transfers between devices, on_device(): lax.all_gather(rollout_rows, ('section', 'cp'), axis=0, tiled=True)  26 us
    dot_general x1, matrix products, on_device(): jnp.einsum('rd,kdc->rkc', normed, qkv_weights, preferred_element_type=jnp...  21.8 us
    all_to_all x1, blocking collectives, on_device(): lax.all_to_all(branch, 'section', split_axis=0, concat_axis=0, tiled=True)  11.7 us
  transfers between devices with their start and end apart: 6, of which 6 were waited for; matrix products, arithmetic and copies ran while one was open for 3% of the time, Pallas kernels for 0%

commit v1 on v0

v1 whole, which is shorter than its diff:
```python
import functools
import math

import jax
import jax.numpy as jnp
from jax import lax
from jax.experimental import pallas as pl
from jax.experimental.pallas import tpu as pltpu
from jax.sharding import PartitionSpec as P

HEAD = 128
MESH = pl.DeviceIdType.MESH


def attend_kernel(
    n_sec, n_cp, n_tp,
    rows_ref, gain_ref, owner_ref, lengths_ref, w_ref,
    att_ref,
    xg, xn, wbuf, buf, part, squares, square_rows, inv_cols, keys, values, pos_q, start_q, pos_k,
    w_sem, row_send, row_recv, sq_send, sq_recv, part_send, part_recv, att_send, att_recv,
):
    sec, cp, tp = lax.axis_index("section"), lax.axis_index("cp"), lax.axis_index("tp")
    blocks, own_rows, width = xg.shape
    tokens = blocks * own_rows
    heads = buf.shape[0]
    per_way = heads // 2
    last = n_tp - 1
    pairs = n_cp // 2
    pair, core = cp // 2, cp % 2
    sibling = cp + 1 - 2 * core
    other = 1 - sec
    mine = sec * n_cp + cp

    def weight_copy(head, kind):
        return pltpu.make_async_copy(
            w_ref.at[0, kind, :, pl.ds(pl.multiple_of(head * HEAD, HEAD), HEAD)],
            wbuf.at[head, :, pl.ds(kind * HEAD, HEAD)],
            w_sem.at[head, kind],
        )

    for i in range(per_way):
        for way in range(2):
            for kind in range(3):
                weight_copy(way * per_way + i, kind).start()

    mates = [((pair + k) % pairs) * 2 + core for k in range(1, pairs)]
    barrier = pltpu.get_barrier_semaphore()
    peers = [{"section": other}, {"cp": sibling}]
    peers += [{"cp": m} for m in mates]
    peers += [{"tp": (tp + k) % n_tp} for k in range(1, n_tp)]
    for peer in peers:
        pl.semaphore_signal(barrier, inc=1, device_id=peer, device_id_type=MESH)
    pl.semaphore_wait(barrier, len(peers))

    sent = []

    def send_rows(src, block, peer):
        copy = pltpu.make_async_remote_copy(
            src_ref=src, dst_ref=xg.at[block], send_sem=row_send.at[len(sent)],
            recv_sem=row_recv.at[block], device_id=peer, device_id_type=MESH,
        )
        copy.start()
        sent.append(copy)

    def wait_rows(block):
        pltpu.make_async_remote_copy(
            src_ref=xg.at[block], dst_ref=xg.at[block], send_sem=row_send.at[0],
            recv_sem=row_recv.at[block], device_id={"cp": sibling}, device_id_type=MESH,
        ).wait_recv()

    send_rows(rows_ref, mine, {"section": other})
    for m in mates:
        send_rows(rows_ref, mine, {"cp": m})
    send_rows(rows_ref, mine, {"cp": sibling})
    xg[mine] = rows_ref[...]

    def positions(shape, dim):
        row = lax.broadcasted_iota(jnp.int32, shape, dim)
        pos = jnp.zeros(shape, jnp.int32)
        for b in range(blocks):
            off = row - owner_ref[b] * own_rows
            pos = jnp.where((off >= 0) & (off < own_rows), off + b * own_rows, pos)
        return pos

    pos = positions((tokens, 1), 0)
    pos_q[...] = pos
    start = jnp.zeros((tokens, 1), jnp.int32)
    end = lengths_ref[0]
    for i in range(1, lengths_ref.shape[0] + 1):
        start = jnp.where(pos >= end, end, start)
        if i < lengths_ref.shape[0]:
            end = end + lengths_ref[i]
    start_q[...] = start
    pos_k[...] = positions((1, tokens), 1)

    across = other * n_cp + cp
    wait_rows(across)
    for m in mates:
        send_rows(xg.at[across], across, {"cp": m})
    send_rows(xg.at[across], across, {"cp": sibling})
    for s in (sec, other):
        for k in range(1, pairs):
            block = s * n_cp + ((pair + pairs - k) % pairs) * 2 + core
            wait_rows(block)
            send_rows(xg.at[block], block, {"cp": sibling})
    for s in (sec, other):
        for k in range(pairs):
            wait_rows(s * n_cp + ((pair + k) % pairs) * 2 + 1 - core)

    def scale_block(block, carry):
        x = xg[block].astype(jnp.float32)
        xn[block] = (x * gain_ref[...]).astype(jnp.bfloat16)
        x = x * x
        total = x[:, :HEAD]
        for t in range(1, width // HEAD):
            total += x[:, t * HEAD:(t + 1) * HEAD]
        squares[block] = total
        return carry

    lax.fori_loop(0, blocks, scale_block, 0)
    summed = jnp.sum(squares[...].reshape(tokens, HEAD).T, axis=0, keepdims=True)
    square_rows[tp] = jnp.broadcast_to(summed, (8, tokens))
    square_copies = []
    for k in range(1, n_tp):
        copy = pltpu.make_async_remote_copy(
            src_ref=square_rows.at[tp], dst_ref=square_rows.at[tp], send_sem=sq_send.at[k - 1],
            recv_sem=sq_recv.at[tp], device_id={"tp": (tp + k) % n_tp}, device_id_type=MESH,
        )
        copy.start()
        square_copies.append(copy)

    step_rows = min(tokens, 512)
    query_rows = min(tokens, 256)

    def chain_copy(ref, send_sem, recv_sem, head, to):
        return pltpu.make_async_remote_copy(
            src_ref=ref.at[head], dst_ref=ref.at[head], send_sem=send_sem.at[head],
            recv_sem=recv_sem.at[head], device_id={"tp": to}, device_id_type=MESH,
        )

    def attend(head):
        def normalise(r, carry):
            at = pl.ds(pl.multiple_of(r * query_rows, query_rows), query_rows)
            inv = inv_cols[at, :]
            keys[at, :] = (buf[head, at, HEAD:2 * HEAD].astype(jnp.float32) * inv).astype(jnp.bfloat16)
            values[at, :] = (buf[head, at, 2 * HEAD:].astype(jnp.float32) * inv).astype(jnp.bfloat16)
            return carry

        lax.fori_loop(0, tokens // query_rows, normalise, 0)

        def queries(r, carry):
            at = pl.ds(pl.multiple_of(r * query_rows, query_rows), query_rows)
            q = (buf[head, at, :HEAD].astype(jnp.float32) * inv_cols[at, :]).astype(jnp.bfloat16)
            scores = lax.dot_general(
                q, keys[...], (((1,), (1,)), ((), ())), preferred_element_type=jnp.float32
            ) * (1.0 / math.sqrt(HEAD))
            spot = pos_k[...]
            allowed = (spot <= pos_q[at, :]) & (spot >= start_q[at, :])
            scores = jnp.where(allowed, scores, -1e30)
            peak = jnp.max(scores, axis=1, keepdims=True)
            weights = jnp.where(allowed, jnp.exp(scores - peak), 0.0)
            total = jnp.sum(weights, axis=1, keepdims=True)
            mixed = jnp.dot(
                weights.astype(jnp.bfloat16), values[...], preferred_element_type=jnp.float32
            )
            att_ref[head, at, :] = (mixed / total).astype(jnp.bfloat16)
            return carry

        lax.fori_loop(0, tokens // query_rows, queries, 0)

    def slot(s, carry):
        @pl.when(s == last)
        def _():
            for k in range(1, n_tp):
                src = (tp + k) % n_tp
                pltpu.make_async_remote_copy(
                    src_ref=square_rows.at[src], dst_ref=square_rows.at[src],
                    send_sem=sq_send.at[0], recv_sem=sq_recv.at[src],
                    device_id={"tp": src}, device_id_type=MESH,
                ).wait_recv()
            total = square_rows[0]
            for k in range(1, n_tp):
                total += square_rows[k]
            inv = lax.rsqrt(total[:1] / (width * n_tp) + 1e-05)
            inv_cols[...] = jnp.broadcast_to(inv, (HEAD, tokens)).T

        for way in range(2):
            place = last - tp if way == 0 else tp
            onward = tp - 1 if way == 0 else tp + 1
            back = tp + 1 if way == 0 else tp - 1
            i = s - place
            head = way * per_way + i

            @pl.when((i >= 0) & (i < per_way))
            def _():
                for kind in range(3):
                    weight_copy(head, kind).wait()

                def multiply(r, c):
                    at = pl.ds(pl.multiple_of(r * step_rows, step_rows), step_rows)
                    held = step_rows // own_rows
                    x = xn[pl.ds(r * held, held)].reshape(step_rows, width)
                    part[at, :] = jnp.dot(x, wbuf[head], preferred_element_type=jnp.float32)
                    return c

                lax.fori_loop(0, tokens // step_rows, multiply, 0)

                @pl.when(place == 0)
                def _():
                    buf[head] = part[...].astype(jnp.bfloat16)

                @pl.when(place > 0)
                def _():
                    chain_copy(buf, part_send, part_recv, head, back).wait_recv()
                    buf[head] = (buf[head].astype(jnp.float32) + part[...]).astype(jnp.bfloat16)

                @pl.when(place < last)
                def _():
                    chain_copy(buf, part_send, part_recv, head, onward).start()

        for way in range(2):
            place = last - tp if way == 0 else tp
            onward = tp - 1 if way == 0 else tp + 1
            back = tp + 1 if way == 0 else tp - 1
            i = s - last - (last - place)
            head = way * per_way + i

            @pl.when((i >= 0) & (i < per_way))
            def _():
                @pl.when(place == last)
                def _():
                    attend(head)

                @pl.when(place < last)
                def _():
                    chain_copy(att_ref, att_send, att_recv, head, onward).wait_recv()

                @pl.when(place > 0)
                def _():
                    chain_copy(att_ref, att_send, att_recv, head, back).start()

        return carry

    lax.fori_loop(0, per_way + 2 * last, slot, 0)

    def finish(i, carry):
        for way in range(2):
            place = last - tp if way == 0 else tp
            onward = tp - 1 if way == 0 else tp + 1
            back = tp + 1 if way == 0 else tp - 1
            head = way * per_way + i

            @pl.when(place < last)
            def _():
                chain_copy(buf, part_send, part_recv, head, onward).wait_send()

            @pl.when(place > 0)
            def _():
                chain_copy(att_ref, att_send, att_recv, head, back).wait_send()

        return carry

    lax.fori_loop(0, per_way, finish, 0)
    for copy in sent + square_copies:
        copy.wait_send()


def on_device(rollout_rows, lengths, block_owner, norm_gain, w_qkv, w_out):
    n_tp, n_cp, n_sec = lax.axis_size("tp"), lax.axis_size("cp"), lax.axis_size("section")
    own_rows, width = rollout_rows.shape
    blocks = n_sec * n_cp
    tokens = own_rows * blocks
    columns = w_qkv.shape[3]
    heads = columns // HEAD
    bf16, f32 = jnp.bfloat16, jnp.float32
    sends = 2 + 2 * n_cp
    vmem = pl.BlockSpec(memory_space=pltpu.VMEM)
    smem = pl.BlockSpec(memory_space=pltpu.SMEM)
    dma = pltpu.SemaphoreType.DMA
    attended = pl.pallas_call(
        functools.partial(attend_kernel, n_sec, n_cp, n_tp),
        out_shape=jax.ShapeDtypeStruct((heads, tokens, HEAD), bf16),
        in_specs=[vmem, vmem, smem, smem, pl.BlockSpec(memory_space=pl.ANY)],
        out_specs=vmem,
        scratch_shapes=[
            pltpu.VMEM((blocks, own_rows, width), bf16),
            pltpu.VMEM((blocks, own_rows, width), bf16),
            pltpu.VMEM((heads, width, 3 * HEAD), bf16),
            pltpu.VMEM((heads, tokens, 3 * HEAD), bf16),
            pltpu.VMEM((tokens, 3 * HEAD), f32),
            pltpu.VMEM((blocks, own_rows, HEAD), f32),
            pltpu.VMEM((n_tp, 8, tokens), f32),
            pltpu.VMEM((tokens, HEAD), f32),
            pltpu.VMEM((tokens, HEAD), bf16),
            pltpu.VMEM((tokens, HEAD), bf16),
            pltpu.VMEM((tokens, 1), jnp.int32),
            pltpu.VMEM((tokens, 1), jnp.int32),
            pltpu.VMEM((1, tokens), jnp.int32),
            dma((heads, 3)),
            dma((sends,)),
            dma((blocks,)),
            dma((n_tp,)),
            dma((n_tp,)),
            dma((heads,)),
            dma((heads,)),
            dma((heads,)),
            dma((heads,)),
        ],
        compiler_params=pltpu.CompilerParams(
            collective_id=0, has_side_effects=True, vmem_limit_bytes=60 * 1024 * 1024
        ),
        name="attend",
    )(rollout_rows, norm_gain, block_owner, lengths, w_qkv)
    attended = attended.transpose(1, 0, 2).reshape(n_sec, n_cp, own_rows, columns)
    ordered = attended.transpose(1, 0, 2, 3).reshape(tokens, columns)
    summed = lax.psum_scatter(
        jnp.dot(ordered, w_out[0], preferred_element_type=f32).astype(bf16),
        "cp", scatter_dimension=0, tiled=True,
    )
    branch = summed.reshape(n_sec, own_rows, width)
    return lax.all_to_all(branch, "section", split_axis=0, concat_axis=0, tiled=True)


def solution(mesh):
    return jax.shard_map(
        on_device,
        mesh=mesh,
        in_specs=(
            P(("section", "cp"), "tp"),
            P(),
            P(),
            P("section", "tp"),
            P("section", None, "tp", "cp"),
            P("section", "cp", "tp"),
        ),
        out_specs=P(None, ("section", "cp"), "tp"),
        check_vma=False,
    )
```

time: 516 us -> 221 us (0.43)
  waiting for transfers between devices: 393 us -> 28 us
  Pallas kernels: 0 us -> 151 us
  matrix products: 40.6 us -> 9.19 us
  local copies, waits for them, and re-layouts: 27.1 us -> 7.79 us
  other arithmetic: 15.7 us -> 0 us
  blocking collectives: 23.4 us -> 11.7 us
    reduce_scatter x2 -> x1, waiting for transfers between devices: 240 us -> 27.9 us  [on_device(): lax.psum_scatter(jnp.dot(ordered, w_out[0], preferred_element_type=f32).a...]
    all_gather x4 -> x0, waiting for transfers between devices: 153 us -> none  [the longest x1 44 us: on_device(): key_part = lax.all_gather(projected[:, 1], 'tp', axis=0, tiled=True)]
    pallas_call x0 -> x1, Pallas kernels: none -> 151 us  [on_device(): pl.pallas_call(functools.partial(attend_kernel, n_sec, n_cp, n_tp), out_s...]
    dot_general x6 -> x1, matrix products: 40.6 us -> 9.19 us  [on_device(): jnp.dot(ordered, w_out[0], preferred_element_type=f32).astype(bf16)]
    gather x4 -> x0, local copies, waits for them, and re-layouts: 14.8 us -> none  [the longest x1 6.27 us: on_device(): rows_in = jnp.take(actor_rows, source, axis=0)]
    psum x1 -> x0, blocking collectives: 11.7 us -> none  [on_device(): total_squares = lax.psum(squares, 'tp')]
    gather x6 -> x0, other arithmetic: 8.59 us -> none  [the longest x2 4.31 us: on_device(): packed_pos = inverse_owner[actor_block] * own_rows + inner]
    unnamed x12 -> x1, local copies, waits for them, and re-layouts: 8.62 us -> 0.79 us
  transfers between devices with their start and end apart: 6 -> 1, of which waited for: 6 -> 1; matrix products, arithmetic and copies ran while one was open for 3% -> 0% of each run, Pallas kernels for 0% -> 0%
where the time goes in v1:
time: 221 us
  Pallas kernels  151 us (68%)
  waiting for transfers between devices  28 us (13%)
  between operations  13.4 us (6%)
  blocking collectives  11.7 us (5%)
  matrix products  9.19 us (4%)
  local copies, waits for them, and re-layouts  7.79 us (4%)
    pallas_call x1, Pallas kernels, on_device(): pl.pallas_call(functools.partial(attend_kernel, n_sec, n_cp, n_tp), out_s...  151 us
    reduce_scatter x1, waiting for transfers between devices, on_device(): lax.psum_scatter(jnp.dot(ordered, w_out[0], preferred_element_type=f32).a...  27.9 us
    all_to_all x1, blocking collectives, on_device(): lax.all_to_all(branch, 'section', split_axis=0, concat_axis=0, tiled=True)  11.7 us
    dot_general x1, matrix products, on_device(): jnp.dot(ordered, w_out[0], preferred_element_type=f32).astype(bf16)  9.19 us
  transfers between devices with their start and end apart: 1, of which 1 were waited for; matrix products, arithmetic and copies ran while one was open for 0% of the time, Pallas kernels for 0%

profile of v1, /device:TPU:0, one launch (start us, length us, event | category | flops | bytes accessed | tf_op | source)
XLA Modules:
  0.0 220.6 jit_solution(1383728692924776691)
XLA Ops:
  6.5 0.0 reduce-scatter.2.cloned.1.call-start
  6.5 150.5 %attend.1 = bf16[16,512,128]{2,1,0:T(8,128)(2,1)} custom-call(bf16[64,2048]{1,0:T(8,128)(2,1)} %rows_ref.1, f32[1,2048]{1,0:T(1,128)} %gain_ref.1, s32[8]{0:T(128)} %owner_ref.1, s32[2]{0:T(128)} %lengths_ref.1, bf16[1,3,2048,2048]{3,2,1,0:T(8,128)(2,1)} %w_ref.1), custom_call_target="tpu_custom_call" | custom-call | tf_op jit(solution)/shard_map/attend/pallas_call | solution.py:280
  157.1 2.9 %copy.7 = bf16[512,16,128]{2,1,0:T(8,128)(2,1)S(1)} copy(bf16[512,16,128]{2,0,1:T(8,128)(2,1)} %bitcast.10) | data formatting | bytes 4194304 | tf_op jit(solution)/shard_map/transpose | solution.py:314
  160.0 2.3 %reshape.9 = bf16[2,4,64,2048]{3,2,1,0:T(8,128)(2,1)} reshape(bf16[512,16,128]{2,1,0:T(8,128)(2,1)S(1)} %copy.7) | data formatting | bytes 4194304 | tf_op jit(solution)/shard_map/reshape | solution.py:314
  162.3 1.7 copy.8
  164.1 9.2 %fusion.2 = bf16[512,2048]{1,0:T(8,128)(2,1)} fusion(bf16[512,2048]{1,0:T(8,128)(2,1)S(1)} %bitcast.12, bf16[1,2048,2048]{2,1,0:T(8,128)(2,1)} %param.11), kind=kOutput, calls=%fused_computation.2 | convolution fusion | flops 4296015872 | bytes 12582912 | tf_op jit(solution)/shard_map/dot_general | solution.py:317
  173.3 0.0 reduce-scatter.2.cloned.1.call-update
  173.3 27.9 %reduce-scatter.2.cloned.1.call-done = bf16[128,2048]{1,0:T(8,128)(2,1)} async-done(((bf16[512,2048]{1,0:T(8,128)(2,1)}), bf16[128,2048]{1,0:T(8,128)(2,1)}) %reduce-scatter.2.cloned.1.call-update) | async-done | bytes 524304 | tf_op jit(solution)/shard_map/reduce_scatter | solution.py:316
  201.2 11.7 %all_to_all.5 = bf16[2,64,2048]{2,1,0:T(8,128)(2,1)S(1)} all-to-all(bf16[2,64,2048]{2,1,0:T(8,128)(2,1)} %bitcast.13), channel_id=1, replica_groups=mesh['section'=2,'cp'=4,'tp'=4] {'section'}, dimensions={0} | all-to-all | bytes 1048576 | tf_op jit(solution)/shard_map/all_to_all | solution.py:321
  212.9 0.8 copy.10
Async XLA Ops:
  6.5 194.7 %reduce-scatter.2.cloned.1.call-start = ((), (), s32[]{:S(2)}) async-start(), calls=%async_computation.2 | async-start | bytes 2621440 | tf_op jit(solution)/shard_map/reduce_scatter | solution.py:316
Sparse Core Ops, SparseCore 0:
  173.4 27.7 reduce-scatter.1

commit v2 on v1

--- a/solution.py
+++ b/solution.py
@@ -14,10 +14,12 @@
 
 def attend_kernel(
     n_sec, n_cp, n_tp,
-    rows_ref, gain_ref, owner_ref, lengths_ref, w_ref,
-    att_ref,
+    rows_ref, gain_ref, owner_ref, lengths_ref, w_ref, w_out_ref,
+    out_ref,
+    att_ref, w_out_buf, lhs, pair_out, pair_in, sums, mate_in, over,
     xg, xn, wbuf, buf, part, squares, square_rows, inv_cols, keys, values, pos_q, start_q, pos_k,
     w_sem, row_send, row_recv, sq_send, sq_recv, part_send, part_recv, att_send, att_recv,
+    out_sem, pair_send, pair_recv, mate_send, mate_recv, home_send, home_recv,
 ):
     sec, cp, tp = lax.axis_index("section"), lax.axis_index("cp"), lax.axis_index("tp")
     blocks, own_rows, width = xg.shape
@@ -42,6 +44,9 @@
         for way in range(2):
             for kind in range(3):
                 weight_copy(way * per_way + i, kind).start()
+
+    out_copy = pltpu.make_async_copy(w_out_ref.at[0], w_out_buf, out_sem)
+    out_copy.start()
 
     mates = [((pair + k) % pairs) * 2 + core for k in range(1, pairs)]
     barrier = pltpu.get_barrier_semaphore()
@@ -129,13 +134,21 @@
         copy.start()
         square_copies.append(copy)
 
-    step_rows = min(tokens, 512)
+    pieces = part_send.shape[1]
+    step_rows = tokens // pieces
     query_rows = min(tokens, 256)
 
-    def chain_copy(ref, send_sem, recv_sem, head, to):
+    def part_copy(head, piece, to):
+        rows = buf.at[head, pl.ds(pl.multiple_of(piece * step_rows, step_rows), step_rows)]
         return pltpu.make_async_remote_copy(
-            src_ref=ref.at[head], dst_ref=ref.at[head], send_sem=send_sem.at[head],
-            recv_sem=recv_sem.at[head], device_id={"tp": to}, device_id_type=MESH,
+            src_ref=rows, dst_ref=rows, send_sem=part_send.at[head, piece],
+            recv_sem=part_recv.at[head, piece], device_id={"tp": to}, device_id_type=MESH,
+        )
+
+    def att_copy(head, to):
+        return pltpu.make_async_remote_copy(
+            src_ref=att_ref.at[head], dst_ref=att_ref.at[head], send_sem=att_send.at[head],
+            recv_sem=att_recv.at[head], device_id={"tp": to}, device_id_type=MESH,
         )
 
     def attend(head):
@@ -163,7 +176,10 @@
             mixed = jnp.dot(
                 weights.astype(jnp.bfloat16), values[...], preferred_element_type=jnp.float32
             )
-            att_ref[head, at, :] = (mixed / total).astype(jnp.bfloat16)
+            held = query_rows // own_rows
+            att_ref[head, pl.ds(r * held, held)] = (
+                (mixed / total).astype(jnp.bfloat16).reshape(held, own_rows, HEAD)
+            )
             return carry
 
         lax.fori_loop(0, tokens // query_rows, queries, 0)
@@ -184,10 +200,10 @@
             inv = lax.rsqrt(total[:1] / (width * n_tp) + 1e-05)
             inv_cols[...] = jnp.broadcast_to(inv, (HEAD, tokens)).T
 
-        for way in range(2):
-            place = last - tp if way == 0 else tp
-            onward = tp - 1 if way == 0 else tp + 1
-            back = tp + 1 if way == 0 else tp - 1
+        def partial_sums(o, c):
+            way = (first + o) % 2
+            place = way * tp + (1 - way) * (last - tp)
+            onward, back = tp + 2 * way - 1, tp - 2 * way + 1
             i = s - place
             head = way * per_way + i
 
@@ -200,28 +216,34 @@
                     at = pl.ds(pl.multiple_of(r * step_rows, step_rows), step_rows)
                     held = step_rows // own_rows
                     x = xn[pl.ds(r * held, held)].reshape(step_rows, width)
-                    part[at, :] = jnp.dot(x, wbuf[head], preferred_element_type=jnp.float32)
+                    part[...] = jnp.dot(x, wbuf[head], preferred_element_type=jnp.float32)
+
+                    @pl.when(place == 0)
+                    def _():
+                        buf[head, at, :] = part[...].astype(jnp.bfloat16)
+
+                    @pl.when(place > 0)
+                    def _():
+                        part_copy(head, r, back).wait_recv()
+                        held_sum = buf[head, at, :].astype(jnp.float32)
+                        buf[head, at, :] = (held_sum + part[...]).astype(jnp.bfloat16)
+
+                    @pl.when(place < last)
+                    def _():
+                        part_copy(head, r, onward).start()
+
                     return c
 
-                lax.fori_loop(0, tokens // step_rows, multiply, 0)
-
-                @pl.when(place == 0)
-                def _():
-                    buf[head] = part[...].astype(jnp.bfloat16)
-
-                @pl.when(place > 0)
-                def _():
-                    chain_copy(buf, part_send, part_recv, head, back).wait_recv()
-                    buf[head] = (buf[head].astype(jnp.float32) + part[...]).astype(jnp.bfloat16)
-
-                @pl.when(place < last)
-                def _():
-                    chain_copy(buf, part_send, part_recv, head, onward).start()
-
-        for way in range(2):
-            place = last - tp if way == 0 else tp
-            onward = tp - 1 if way == 0 else tp + 1
-            back = tp + 1 if way == 0 else tp - 1
+                lax.fori_loop(0, pieces, multiply, 0)
+
+            return c
+
+        lax.fori_loop(0, 2, partial_sums, 0)
+
+        def attended_rows(o, c):
+            way = (first + 1 + o) % 2
+            place = way * tp + (1 - way) * (last - tp)
+            onward, back = tp + 2 * way - 1, tp - 2 * way + 1
             i = s - last - (last - place)
             head = way * per_way + i
 
@@ -233,15 +255,92 @@
 
                 @pl.when(place < last)
                 def _():
-                    chain_copy(att_ref, att_send, att_recv, head, onward).wait_recv()
+                    att_copy(head, onward).wait_recv()
 
                 @pl.when(place > 0)
                 def _():
-                    chain_copy(att_ref, att_send, att_recv, head, back).start()
-
+                    att_copy(head, back).start()
+
+            return c
+
+        lax.fori_loop(0, 2, attended_rows, 0)
         return carry
 
+    first = 1 - (2 * tp) // n_tp
     lax.fori_loop(0, per_way + 2 * last, slot, 0)
+
+    out_copy.wait()
+    columns = lhs.shape[1]
+    tile = min(width, 512)
+
+    def project(section, to_core, target, arrived):
+        for k in range(pairs):
+            block = section * n_cp + 2 * k + to_core
+            for h in range(heads):
+                lhs[k * own_rows:(k + 1) * own_rows, h * HEAD:(h + 1) * HEAD] = att_ref[h, block]
+
+        def one_tile(t, c):
+            at = pl.ds(pl.multiple_of(t * tile, tile), tile)
+            product = jnp.dot(
+                lhs[...], w_out_buf[:, at], preferred_element_type=jnp.float32
+            ).reshape(pairs, own_rows, tile)
+            if arrived is not None:
+                product += arrived[section, :, :, at].astype(jnp.float32)
+            target[section, :, :, at] = product.astype(jnp.bfloat16)
+            return c
+
+        lax.fori_loop(0, width // tile, one_tile, 0)
+
+    def pair_copy(section):
+        return pltpu.make_async_remote_copy(
+            src_ref=pair_out.at[section], dst_ref=pair_in.at[section],
+            send_sem=pair_send.at[section], recv_sem=pair_recv.at[section],
+            device_id={"cp": sibling}, device_id_type=MESH,
+        )
+
+    def mate_copy(section, k):
+        to = (pair + k) % pairs
+        return pltpu.make_async_remote_copy(
+            src_ref=sums.at[section, to], dst_ref=mate_in.at[section, pair],
+            send_sem=mate_send.at[section, to], recv_sem=mate_recv.at[section, pair],
+            device_id={"cp": 2 * to + core}, device_id_type=MESH,
+        )
+
+    def wait_mate(section, k):
+        src = (pair + pairs - k) % pairs
+        pltpu.make_async_remote_copy(
+            src_ref=mate_in.at[section, src], dst_ref=mate_in.at[section, src],
+            send_sem=mate_send.at[section, src], recv_sem=mate_recv.at[section, src],
+            device_id={"cp": 2 * src + core}, device_id_type=MESH,
+        ).wait_recv()
+
+    def total_of(section):
+        total = sums[section, pair].astype(jnp.float32)
+        for k in range(1, pairs):
+            wait_mate(section, k)
+            total += mate_in[section, (pair + pairs - k) % pairs].astype(jnp.float32)
+        return total.astype(jnp.bfloat16)
+
+    for section in (other, sec):
+        project(section, 1 - core, pair_out, None)
+        pair_copy(section).start()
+        pair_copy(section).wait_recv()
+        project(section, core, sums, pair_in)
+        for k in range(1, pairs):
+            mate_copy(section, k).start()
+
+    over[...] = total_of(other)
+    home = pltpu.make_async_remote_copy(
+        src_ref=over, dst_ref=out_ref.at[sec], send_sem=home_send, recv_sem=home_recv,
+        device_id={"section": other}, device_id_type=MESH,
+    )
+    home.start()
+    out_ref[sec] = total_of(sec)
+    home.wait()
+    for section in (other, sec):
+        pair_copy(section).wait_send()
+        for k in range(1, pairs):
+            mate_copy(section, k).wait_send()
 
     def finish(i, carry):
         for way in range(2):
@@ -252,11 +351,12 @@
 
             @pl.when(place < last)
             def _():
-                chain_copy(buf, part_send, part_recv, head, onward).wait_send()
+                for piece in range(pieces):
+                    part_copy(head, piece, onward).wait_send()
 
             @pl.when(place > 0)
             def _():
-                chain_copy(att_ref, att_send, att_recv, head, back).wait_send()
+                att_copy(head, back).wait_send()
 
         return carry
 
@@ -277,17 +377,28 @@
     vmem = pl.BlockSpec(memory_space=pltpu.VMEM)
     smem = pl.BlockSpec(memory_space=pltpu.SMEM)
     dma = pltpu.SemaphoreType.DMA
-    attended = pl.pallas_call(
+    pairs = n_cp // 2
+    pieces = max(2, tokens // 512)
+    exchange = pltpu.VMEM((n_sec, pairs, own_rows, width), bf16)
+    return pl.pallas_call(
         functools.partial(attend_kernel, n_sec, n_cp, n_tp),
-        out_shape=jax.ShapeDtypeStruct((heads, tokens, HEAD), bf16),
-        in_specs=[vmem, vmem, smem, smem, pl.BlockSpec(memory_space=pl.ANY)],
+        out_shape=jax.ShapeDtypeStruct((n_sec, own_rows, width), bf16),
+        in_specs=[vmem, vmem, smem, smem] + [pl.BlockSpec(memory_space=pl.ANY)] * 2,
         out_specs=vmem,
         scratch_shapes=[
+            pltpu.VMEM((heads, blocks, own_rows, HEAD), bf16),
+            pltpu.VMEM((columns, width), bf16),
+            pltpu.VMEM((pairs * own_rows, columns), bf16),
+            exchange,
+            exchange,
+            exchange,
+            exchange,
+            pltpu.VMEM((own_rows, width), bf16),
             pltpu.VMEM((blocks, own_rows, width), bf16),
             pltpu.VMEM((blocks, own_rows, width), bf16),
             pltpu.VMEM((heads, width, 3 * HEAD), bf16),
             pltpu.VMEM((heads, tokens, 3 * HEAD), bf16),
-            pltpu.VMEM((tokens, 3 * HEAD), f32),
+            pltpu.VMEM((tokens // pieces, 3 * HEAD), f32),
             pltpu.VMEM((blocks, own_rows, HEAD), f32),
             pltpu.VMEM((n_tp, 8, tokens), f32),
             pltpu.VMEM((tokens, HEAD), f32),
@@ -301,24 +412,23 @@
             dma((blocks,)),
             dma((n_tp,)),
             dma((n_tp,)),
+            dma((heads, pieces)),
+            dma((heads, pieces)),
             dma((heads,)),
             dma((heads,)),
-            dma((heads,)),
-            dma((heads,)),
+            dma,
+            dma((n_sec,)),
+            dma((n_sec,)),
+            dma((n_sec, pairs)),
+            dma((n_sec, pairs)),
+            dma,
+            dma,
         ],
         compiler_params=pltpu.CompilerParams(
-            collective_id=0, has_side_effects=True, vmem_limit_bytes=60 * 1024 * 1024
+            collective_id=0, has_side_effects=True, vmem_limit_bytes=62 * 1024 * 1024
         ),
         name="attend",
-    )(rollout_rows, norm_gain, block_owner, lengths, w_qkv)
-    attended = attended.transpose(1, 0, 2).reshape(n_sec, n_cp, own_rows, columns)
-    ordered = attended.transpose(1, 0, 2, 3).reshape(tokens, columns)
-    summed = lax.psum_scatter(
-        jnp.dot(ordered, w_out[0], preferred_element_type=f32).astype(bf16),
-        "cp", scatter_dimension=0, tiled=True,
-    )
-    branch = summed.reshape(n_sec, own_rows, width)
-    return lax.all_to_all(branch, "section", split_axis=0, concat_axis=0, tiled=True)
+    )(rollout_rows, norm_gain, block_owner, lengths, w_qkv, w_out)
 
 
 def solution(mesh):

time: 221 us -> 165 us (0.75)
  waiting for transfers between devices: 28 us -> 0 us
  between operations: 13.4 us -> 0.01 us
  Pallas kernels: 151 us -> 163 us
  blocking collectives: 11.7 us -> 0 us
  matrix products: 9.19 us -> 0 us
  local copies, waits for them, and re-layouts: 7.79 us -> 1.88 us
    reduce_scatter x1 -> x0, waiting for transfers between devices: 27.9 us -> none  [on_device(): lax.psum_scatter(jnp.dot(ordered, w_out[0], preferred_element_type=f32).a...]
    pallas_call x1, Pallas kernels: 151 us -> 163 us  [on_device(): pl.pallas_call(functools.partial(attend_kernel, n_sec, n_cp, n_tp), out_s...]
    all_to_all x1 -> x0, blocking collectives: 11.7 us -> none  [on_device(): lax.all_to_all(branch, 'section', split_axis=0, concat_axis=0, tiled=True)]
    dot_general x1 -> x0, matrix products: 9.19 us -> none  [on_device(): jnp.dot(ordered, w_out[0], preferred_element_type=f32).astype(bf16)]
    transpose x2 -> x0, local copies, waits for them, and re-layouts: 4.67 us -> none  [the longest x1 2.94 us: on_device(): attended.transpose(1, 0, 2).reshape(n_sec, n_cp, own_rows, columns)]
    reshape x1 -> x0, local copies, waits for them, and re-layouts: 2.32 us -> none  [on_device(): attended.transpose(1, 0, 2).reshape(n_sec, n_cp, own_rows, columns)]
  transfers between devices with their start and end apart: 1 -> 0, of which waited for: 1 -> 0; matrix products, arithmetic and copies ran while one was open for 0% -> 0% of each run, Pallas kernels for 0% -> 0%
where the time goes in v2:
time: 165 us; the launch traced here: 164 us
  Pallas kernels  163 us (99%)
  local copies, waits for them, and re-layouts  1.88 us (1%)
    pallas_call x1, Pallas kernels, on_device(): pl.pallas_call(functools.partial(attend_kernel, n_sec, n_cp, n_tp), out_s...  163 us

profile of v2, /device:TPU:0, one launch (start us, length us, event | category | flops | bytes accessed | tf_op | source)
XLA Modules:
  0.0 164.4 jit_solution(9871983920087810025)
XLA Ops:
  0.0 162.5 %attend.1 = bf16[2,64,2048]{2,1,0:T(8,128)(2,1)} custom-call(bf16[64,2048]{1,0:T(8,128)(2,1)} %rows_ref.1, f32[1,2048]{1,0:T(1,128)} %gain_ref.1, s32[8]{0:T(128)} %owner_ref.1, s32[2]{0:T(128)} %lengths_ref.1, bf16[1,3,2048,2048]{3,2,1,0:T(8,128)(2,1)} %w_ref.1, bf16[1,2048,2048]{2,1,0:T(8,128)(2,1)} %w_out_ref.1), custom_call_target="tpu_custom_call" | custom-call | tf_op jit(solution)/shard_map/attend/pallas_call | solution.py:383
  162.5 1.9 %copy.8 = bf16[2,64,2048]{2,1,0:T(8,128)(2,1)} copy(bf16[2,64,2048]{2,1,0:T(8,128)(2,1)} %attend.1) | data formatting | bytes 1048576

commit v3 on v2

--- a/solution.py
+++ b/solution.py
@@ -98,21 +98,40 @@
     start_q[...] = start
     pos_k[...] = positions((1, tokens), 1)
 
-    across = other * n_cp + cp
-    wait_rows(across)
-    for m in mates:
-        send_rows(xg.at[across], across, {"cp": m})
-    send_rows(xg.at[across], across, {"cp": sibling})
-    for s in (sec, other):
-        for k in range(1, pairs):
-            block = s * n_cp + ((pair + pairs - k) % pairs) * 2 + core
-            wait_rows(block)
-            send_rows(xg.at[block], block, {"cp": sibling})
-    for s in (sec, other):
-        for k in range(pairs):
-            wait_rows(s * n_cp + ((pair + k) % pairs) * 2 + 1 - core)
-
-    def scale_block(block, carry):
+    pieces = n_sec * pairs
+    step_rows = 2 * own_rows
+    query_rows = min(tokens, 256)
+    att_pieces = tokens // query_rows
+    group = min(4, per_way)
+    lead = group * pieces
+    first = 1 - (2 * tp) // n_tp
+
+    def piece_block(q):
+        section = sec + (q % 2) * (other - sec)
+        return section * n_cp + 2 * ((pair + pairs - q // 2) % pairs)
+
+    def part_copy(head, q, to):
+        rows = buf.at[head, pl.ds(pl.multiple_of(piece_block(q) * own_rows, step_rows), step_rows)]
+        return pltpu.make_async_remote_copy(
+            src_ref=rows, dst_ref=rows, send_sem=part_send.at[head, q],
+            recv_sem=part_recv.at[head, q], device_id={"tp": to}, device_id_type=MESH,
+        )
+
+    def att_copy(head, r, to):
+        held = query_rows // own_rows
+        rows = att_ref.at[head, pl.ds(r * held, held)]
+        return pltpu.make_async_remote_copy(
+            src_ref=rows, dst_ref=rows, send_sem=att_send.at[head, r],
+            recv_sem=att_recv.at[head, r], device_id={"tp": to}, device_id_type=MESH,
+        )
+
+    def multiply(head, q):
+        block = piece_block(q)
+        x = xn[pl.ds(block, 2)].reshape(step_rows, width)
+        part[...] = jnp.dot(x, wbuf[head], preferred_element_type=jnp.float32)
+        return pl.ds(pl.multiple_of(block * own_rows, step_rows), step_rows)
+
+    def scale_block(block):
         x = xg[block].astype(jnp.float32)
         xn[block] = (x * gain_ref[...]).astype(jnp.bfloat16)
         x = x * x
@@ -120,9 +139,50 @@
         for t in range(1, width // HEAD):
             total += x[:, t * HEAD:(t + 1) * HEAD]
         squares[block] = total
-        return carry
-
-    lax.fori_loop(0, blocks, scale_block, 0)
+
+    def begin(q):
+        def scale(k, c):
+            scale_block(piece_block(q) + k)
+            return c
+
+        lax.fori_loop(0, 2, scale, 0)
+
+        @pl.when((tp == 0) | (tp == last))
+        def _():
+            def one_head(j, c):
+                head = first * per_way + j
+                if q == 0:
+                    for kind in range(3):
+                        weight_copy(head, kind).wait()
+                at = multiply(head, q)
+                buf[head, at, :] = part[...].astype(jnp.bfloat16)
+                part_copy(head, q, tp + 2 * first - 1).start()
+                return c
+
+            lax.fori_loop(0, group, one_head, 0)
+
+    across = other * n_cp + cp
+    wait_rows(mine + 1 - 2 * core)
+    begin(0)
+    wait_rows(across)
+    for m in mates:
+        send_rows(xg.at[across], across, {"cp": m})
+    send_rows(xg.at[across], across, {"cp": sibling})
+    for k in range(1, pairs):
+        block = sec * n_cp + ((pair + pairs - k) % pairs) * 2 + core
+        wait_rows(block)
+        send_rows(xg.at[block], block, {"cp": sibling})
+    wait_rows(across + 1 - 2 * core)
+    begin(1)
+    for k in range(1, pairs):
+        block = other * n_cp + ((pair + pairs - k) % pairs) * 2 + core
+        wait_rows(block)
+        send_rows(xg.at[block], block, {"cp": sibling})
+    for k in range(1, pairs):
+        for i, side in enumerate((sec, other)):
+            wait_rows(side * n_cp + ((pair + pairs - k) % pairs) * 2 + 1 - core)
+            begin(2 * k + i)
+
     summed = jnp.sum(squares[...].reshape(tokens, HEAD).T, axis=0, keepdims=True)
     square_rows[tp] = jnp.broadcast_to(summed, (8, tokens))
     square_copies = []
@@ -134,24 +194,7 @@
         copy.start()
         square_copies.append(copy)
 
-    pieces = part_send.shape[1]
-    step_rows = tokens // pieces
-    query_rows = min(tokens, 256)
-
-    def part_copy(head, piece, to):
-        rows = buf.at[head, pl.ds(pl.multiple_of(piece * step_rows, step_rows), step_rows)]
-        return pltpu.make_async_remote_copy(
-            src_ref=rows, dst_ref=rows, send_sem=part_send.at[head, piece],
-            recv_sem=part_recv.at[head, piece], device_id={"tp": to}, device_id_type=MESH,
-        )
-
-    def att_copy(head, to):
-        return pltpu.make_async_remote_copy(
-            src_ref=att_ref.at[head], dst_ref=att_ref.at[head], send_sem=att_send.at[head],
-            recv_sem=att_recv.at[head], device_id={"tp": to}, device_id_type=MESH,
-        )
-
-    def attend(head):
+    def attend(head, back):
         def normalise(r, carry):
             at = pl.ds(pl.multiple_of(r * query_rows, query_rows), query_rows)
             inv = inv_cols[at, :]
@@ -180,12 +223,13 @@
             att_ref[head, pl.ds(r * held, held)] = (
                 (mixed / total).astype(jnp.bfloat16).reshape(held, own_rows, HEAD)
             )
+            att_copy(head, r, back).start()
             return carry
 
         lax.fori_loop(0, tokens // query_rows, queries, 0)
 
     def slot(s, carry):
-        @pl.when(s == last)
+        @pl.when(s == 2)
         def _():
             for k in range(1, n_tp):
                 src = (tp + k) % n_tp
@@ -204,37 +248,47 @@
             way = (first + o) % 2
             place = way * tp + (1 - way) * (last - tp)
             onward, back = tp + 2 * way - 1, tp - 2 * way + 1
-            i = s - place
-            head = way * per_way + i
-
-            @pl.when((i >= 0) & (i < per_way))
+
+            @pl.when(place == 0)
             def _():
-                for kind in range(3):
-                    weight_copy(head, kind).wait()
-
-                def multiply(r, c):
-                    at = pl.ds(pl.multiple_of(r * step_rows, step_rows), step_rows)
-                    held = step_rows // own_rows
-                    x = xn[pl.ds(r * held, held)].reshape(step_rows, width)
-                    part[...] = jnp.dot(x, wbuf[head], preferred_element_type=jnp.float32)
-
-                    @pl.when(place == 0)
+                i = s + lead
+
+                @pl.when(i < steps)
+                def _():
+                    head, q = decode(i)
+                    head = way * per_way + head
+
+                    @pl.when(q == 0)
                     def _():
-                        buf[head, at, :] = part[...].astype(jnp.bfloat16)
-
-                    @pl.when(place > 0)
+                        for kind in range(3):
+                            weight_copy(head, kind).wait()
+
+                    at = multiply(head, q)
+                    buf[head, at, :] = part[...].astype(jnp.bfloat16)
+                    part_copy(head, q, onward).start()
+
+            @pl.when(place > 0)
+            def _():
+                i = s - (place - 1) * hop
+
+                @pl.when((i >= 0) & (i < steps))
+                def _():
+                    head, q = decode(i)
+                    head = way * per_way + head
+
+                    @pl.when(q == 0)
                     def _():
-                        part_copy(head, r, back).wait_recv()
-                        held_sum = buf[head, at, :].astype(jnp.float32)
-                        buf[head, at, :] = (held_sum + part[...]).astype(jnp.bfloat16)
+                        for kind in range(3):
+                            weight_copy(head, kind).wait()
+
+                    at = multiply(head, q)
+                    part_copy(head, q, back).wait_recv()
+                    held_sum = buf[head, at, :].astype(jnp.float32)
+                    buf[head, at, :] = (held_sum + part[...]).astype(jnp.bfloat16)
 
                     @pl.when(place < last)
                     def _():
-                        part_copy(head, r, onward).start()
-
-                    return c
-
-                lax.fori_loop(0, pieces, multiply, 0)
+                        part_copy(head, q, onward).start()
 
             return c
 
@@ -244,30 +298,48 @@
             way = (first + 1 + o) % 2
             place = way * tp + (1 - way) * (last - tp)
             onward, back = tp + 2 * way - 1, tp - 2 * way + 1
-            i = s - last - (last - place)
-            head = way * per_way + i
-
-            @pl.when((i >= 0) & (i < per_way))
+            i = s - (last - 1) * hop - (last - place) * back_hop
+
+            @pl.when((i >= 0) & (i < steps))
             def _():
-                @pl.when(place == last)
+                head, q = decode(i)
+                head = way * per_way + head
+
+                @pl.when(q == pieces - 1)
                 def _():
-                    attend(head)
-
-                @pl.when(place < last)
-                def _():
-                    att_copy(head, onward).wait_recv()
-
-                @pl.when(place > 0)
-                def _():
-                    att_copy(head, back).start()
+                    @pl.when(place == last)
+                    def _():
+                        attend(head, back)
+
+                    @pl.when(place < last)
+                    def _():
+                        def pass_on(r, d):
+                            att_copy(head, r, onward).wait_recv()
+
+                            @pl.when(place > 0)
+                            def _():
+                                att_copy(head, r, back).start()
+
+                            return d
+
+                        lax.fori_loop(0, att_pieces, pass_on, 0)
 
             return c
 
         lax.fori_loop(0, 2, attended_rows, 0)
         return carry
 
-    first = 1 - (2 * tp) // n_tp
-    lax.fori_loop(0, per_way + 2 * last, slot, 0)
+    steps = per_way * pieces
+    hop, back_hop = 3, 3
+
+    def decode(i):
+        early = i < lead
+        return (
+            jnp.where(early, i % group, i // pieces),
+            jnp.where(early, i // group, i % pieces),
+        )
+
+    lax.fori_loop(0, steps + (last - 1) * hop + last * back_hop, slot, 0)
 
     out_copy.wait()
     columns = lhs.shape[1]
@@ -356,7 +428,8 @@
 
             @pl.when(place > 0)
             def _():
-                att_copy(head, back).wait_send()
+                for r in range(att_pieces):
+                    att_copy(head, r, back).wait_send()
 
         return carry
 
@@ -378,7 +451,8 @@
     smem = pl.BlockSpec(memory_space=pltpu.SMEM)
     dma = pltpu.SemaphoreType.DMA
     pairs = n_cp // 2
-    pieces = max(2, tokens // 512)
+    pieces = n_sec * pairs
+    att_pieces = tokens // min(tokens, 256)
     exchange = pltpu.VMEM((n_sec, pairs, own_rows, width), bf16)
     return pl.pallas_call(
         functools.partial(attend_kernel, n_sec, n_cp, n_tp),
@@ -398,7 +472,7 @@
             pltpu.VMEM((blocks, own_rows, width), bf16),
             pltpu.VMEM((heads, width, 3 * HEAD), bf16),
             pltpu.VMEM((heads, tokens, 3 * HEAD), bf16),
-            pltpu.VMEM((tokens // pieces, 3 * HEAD), f32),
+            pltpu.VMEM((2 * own_rows, 3 * HEAD), f32),
             pltpu.VMEM((blocks, own_rows, HEAD), f32),
             pltpu.VMEM((n_tp, 8, tokens), f32),
             pltpu.VMEM((tokens, HEAD), f32),
@@ -414,8 +488,8 @@
             dma((n_tp,)),
             dma((heads, pieces)),
             dma((heads, pieces)),
-            dma((heads,)),
-            dma((heads,)),
+            dma((heads, att_pieces)),
+            dma((heads, att_pieces)),
             dma,
             dma((n_sec,)),
             dma((n_sec,)),

time: 165 us -> 167 us (1.012)
  Pallas kernels: 163 us -> 165 us
    pallas_call x1, Pallas kernels: 163 us -> 165 us  [on_device(): pl.pallas_call(functools.partial(attend_kernel, n_sec, n_cp, n_tp), out_s...]
where the time goes in v3:
time: 167 us
  Pallas kernels  165 us (99%)
  local copies, waits for them, and re-layouts  1.88 us (1%)
    pallas_call x1, Pallas kernels, on_device(): pl.pallas_call(functools.partial(attend_kernel, n_sec, n_cp, n_tp), out_s...  165 us

profile of v3, /device:TPU:0, one launch (start us, length us, event | category | flops | bytes accessed | tf_op | source)
XLA Modules:
  0.0 166.5 jit_solution(9656566424189167602)
XLA Ops:
  0.0 164.6 %attend.1 = bf16[2,64,2048]{2,1,0:T(8,128)(2,1)} custom-call(bf16[64,2048]{1,0:T(8,128)(2,1)} %rows_ref.1, f32[1,2048]{1,0:T(1,128)} %gain_ref.1, s32[8]{0:T(128)} %owner_ref.1, s32[2]{0:T(128)} %lengths_ref.1, bf16[1,3,2048,2048]{3,2,1,0:T(8,128)(2,1)} %w_ref.1, bf16[1,2048,2048]{2,1,0:T(8,128)(2,1)} %w_out_ref.1), custom_call_target="tpu_custom_call" | custom-call | tf_op jit(solution)/shard_map/attend/pallas_call | solution.py:457
  164.6 1.9 %copy.8 = bf16[2,64,2048]{2,1,0:T(8,128)(2,1)} copy(bf16[2,64,2048]{2,1,0:T(8,128)(2,1)} %attend.1) | data formatting | bytes 1048576

commit v4 on v3

--- a/solution.py
+++ b/solution.py
@@ -102,7 +102,7 @@
     step_rows = 2 * own_rows
     query_rows = min(tokens, 256)
     att_pieces = tokens // query_rows
-    group = min(4, per_way)
+    group = min(2, per_way)
     lead = group * pieces
     first = 1 - (2 * tp) // n_tp
 
@@ -251,9 +251,9 @@
 
             @pl.when(place == 0)
             def _():
-                i = s + lead
-
-                @pl.when(i < steps)
+                i = s + ahead
+
+                @pl.when((i >= lead) & (i < steps))
                 def _():
                     head, q = decode(i)
                     head = way * per_way + head
@@ -330,7 +330,7 @@
         return carry
 
     steps = per_way * pieces
-    hop, back_hop = 3, 3
+    hop, back_hop, ahead = 3, 6, min(4, lead)
 
     def decode(i):
         early = i < lead

time: 167 us -> 154 us (0.922)
  Pallas kernels: 165 us -> 152 us
    pallas_call x1, Pallas kernels: 165 us -> 152 us  [on_device(): pl.pallas_call(functools.partial(attend_kernel, n_sec, n_cp, n_tp), out_s...]
where the time goes in v4:
time: 154 us
  Pallas kernels  152 us (99%)
  local copies, waits for them, and re-layouts  1.88 us (1%)
    pallas_call x1, Pallas kernels, on_device(): pl.pallas_call(functools.partial(attend_kernel, n_sec, n_cp, n_tp), out_s...  152 us

profile of v4, /device:TPU:0, one launch (start us, length us, event | category | flops | bytes accessed | tf_op | source)
XLA Modules:
  0.0 153.8 jit_solution(7222660359960846391)
XLA Ops:
  0.0 151.9 %attend.1 = bf16[2,64,2048]{2,1,0:T(8,128)(2,1)} custom-call(bf16[64,2048]{1,0:T(8,128)(2,1)} %rows_ref.1, f32[1,2048]{1,0:T(1,128)} %gain_ref.1, s32[8]{0:T(128)} %owner_ref.1, s32[2]{0:T(128)} %lengths_ref.1, bf16[1,3,2048,2048]{3,2,1,0:T(8,128)(2,1)} %w_ref.1, bf16[1,2048,2048]{2,1,0:T(8,128)(2,1)} %w_out_ref.1), custom_call_target="tpu_custom_call" | custom-call | tf_op jit(solution)/shard_map/attend/pallas_call | solution.py:457
  151.9 1.9 %copy.8 = bf16[2,64,2048]{2,1,0:T(8,128)(2,1)} copy(bf16[2,64,2048]{2,1,0:T(8,128)(2,1)} %attend.1) | data formatting | bytes 1048576

commit v5 on v4

--- a/solution.py
+++ b/solution.py
@@ -330,7 +330,7 @@
         return carry
 
     steps = per_way * pieces
-    hop, back_hop, ahead = 3, 6, min(4, lead)
+    hop, back_hop, ahead = 3, 4, min(3, lead)
 
     def decode(i):
         early = i < lead
@@ -342,77 +342,101 @@
     lax.fori_loop(0, steps + (last - 1) * hop + last * back_hop, slot, 0)
 
     out_copy.wait()
-    columns = lhs.shape[1]
-    tile = min(width, 512)
-
-    def project(section, to_core, target, arrived):
+    half_width = width // 2
+    tile = min(half_width, 512)
+
+    def gather_heads(section, to_core):
         for k in range(pairs):
             block = section * n_cp + 2 * k + to_core
             for h in range(heads):
-                lhs[k * own_rows:(k + 1) * own_rows, h * HEAD:(h + 1) * HEAD] = att_ref[h, block]
-
+                lhs[section, to_core, k * own_rows:(k + 1) * own_rows, h * HEAD:(h + 1) * HEAD] = (
+                    att_ref[h, block]
+                )
+
+    def project(section, half, to_core, target, arrived):
         def one_tile(t, c):
             at = pl.ds(pl.multiple_of(t * tile, tile), tile)
+            columns = pl.ds(pl.multiple_of(half * half_width + t * tile, tile), tile)
             product = jnp.dot(
-                lhs[...], w_out_buf[:, at], preferred_element_type=jnp.float32
+                lhs[section, to_core], w_out_buf[:, columns], preferred_element_type=jnp.float32
             ).reshape(pairs, own_rows, tile)
             if arrived is not None:
-                product += arrived[section, :, :, at].astype(jnp.float32)
-            target[section, :, :, at] = product.astype(jnp.bfloat16)
+                product += arrived[section, half, :, :, at].astype(jnp.float32)
+            target[section, half, :, :, at] = product.astype(jnp.bfloat16)
             return c
 
-        lax.fori_loop(0, width // tile, one_tile, 0)
-
-    def pair_copy(section):
+        lax.fori_loop(0, half_width // tile, one_tile, 0)
+
+    def pair_copy(section, half):
         return pltpu.make_async_remote_copy(
-            src_ref=pair_out.at[section], dst_ref=pair_in.at[section],
-            send_sem=pair_send.at[section], recv_sem=pair_recv.at[section],
+            src_ref=pair_out.at[section, half], dst_ref=pair_in.at[section, half],
+            send_sem=pair_send.at[section, half], recv_sem=pair_recv.at[section, half],
             device_id={"cp": sibling}, device_id_type=MESH,
         )
 
-    def mate_copy(section, k):
+    def mate_copy(section, half, k):
         to = (pair + k) % pairs
         return pltpu.make_async_remote_copy(
-            src_ref=sums.at[section, to], dst_ref=mate_in.at[section, pair],
-            send_sem=mate_send.at[section, to], recv_sem=mate_recv.at[section, pair],
+            src_ref=sums.at[section, half, to], dst_ref=mate_in.at[section, half, pair],
+            send_sem=mate_send.at[section, half, to], recv_sem=mate_recv.at[section, half, pair],
             device_id={"cp": 2 * to + core}, device_id_type=MESH,
         )
 
-    def wait_mate(section, k):
+    def wait_mate(section, half, k):
         src = (pair + pairs - k) % pairs
         pltpu.make_async_remote_copy(
-            src_ref=mate_in.at[section, src], dst_ref=mate_in.at[section, src],
-            send_sem=mate_send.at[section, src], recv_sem=mate_recv.at[section, src],
+            src_ref=mate_in.at[section, half, src], dst_ref=mate_in.at[section, half, src],
+            send_sem=mate_send.at[section, half, src], recv_sem=mate_recv.at[section, half, src],
             device_id={"cp": 2 * src + core}, device_id_type=MESH,
         ).wait_recv()
 
-    def total_of(section):
-        total = sums[section, pair].astype(jnp.float32)
+    def total_of(section, half):
+        total = sums[section, half, pair].astype(jnp.float32)
         for k in range(1, pairs):
-            wait_mate(section, k)
-            total += mate_in[section, (pair + pairs - k) % pairs].astype(jnp.float32)
+            wait_mate(section, half, k)
+            total += mate_in[section, half, (pair + pairs - k) % pairs].astype(jnp.float32)
         return total.astype(jnp.bfloat16)
 
-    for section in (other, sec):
-        project(section, 1 - core, pair_out, None)
-        pair_copy(section).start()
-        pair_copy(section).wait_recv()
-        project(section, core, sums, pair_in)
+    def to_sibling(section, half):
+        if half == 0:
+            gather_heads(section, 1 - core)
+        project(section, half, 1 - core, pair_out, None)
+        pair_copy(section, half).start()
+
+    def to_mates(section, half):
+        if half == 0:
+            gather_heads(section, core)
+        pair_copy(section, half).wait_recv()
+        project(section, half, core, sums, pair_in)
         for k in range(1, pairs):
-            mate_copy(section, k).start()
-
-    over[...] = total_of(other)
-    home = pltpu.make_async_remote_copy(
-        src_ref=over, dst_ref=out_ref.at[sec], send_sem=home_send, recv_sem=home_recv,
-        device_id={"section": other}, device_id_type=MESH,
-    )
-    home.start()
-    out_ref[sec] = total_of(sec)
-    home.wait()
-    for section in (other, sec):
-        pair_copy(section).wait_send()
+            mate_copy(section, half, k).start()
+
+    order = [(other, 0), (other, 1), (sec, 0), (sec, 1)]
+    to_sibling(*order[0])
+    for n, spot in enumerate(order):
+        if n + 1 < len(order):
+            to_sibling(*order[n + 1])
+        to_mates(*spot)
+
+    homes = []
+    for half in range(2):
+        over[half] = total_of(other, half)
+        home = pltpu.make_async_remote_copy(
+            src_ref=over.at[half],
+            dst_ref=out_ref.at[sec, :, pl.ds(half * half_width, half_width)],
+            send_sem=home_send.at[half], recv_sem=home_recv.at[half],
+            device_id={"section": other}, device_id_type=MESH,
+        )
+        home.start()
+        homes.append(home)
+    for half in range(2):
+        out_ref[sec, :, half * half_width:(half + 1) * half_width] = total_of(sec, half)
+    for home in homes:
+        home.wait()
+    for section, half in order:
+        pair_copy(section, half).wait_send()
         for k in range(1, pairs):
-            mate_copy(section, k).wait_send()
+            mate_copy(section, half, k).wait_send()
 
     def finish(i, carry):
         for way in range(2):
@@ -453,7 +477,7 @@
     pairs = n_cp // 2
     pieces = n_sec * pairs
     att_pieces = tokens // min(tokens, 256)
-    exchange = pltpu.VMEM((n_sec, pairs, own_rows, width), bf16)
+    exchange = pltpu.VMEM((n_sec, 2, pairs, own_rows, width // 2), bf16)
     return pl.pallas_call(
         functools.partial(attend_kernel, n_sec, n_cp, n_tp),
         out_shape=jax.ShapeDtypeStruct((n_sec, own_rows, width), bf16),
@@ -462,12 +486,12 @@
         scratch_shapes=[
             pltpu.VMEM((heads, blocks, own_rows, HEAD), bf16),
             pltpu.VMEM((columns, width), bf16),
-            pltpu.VMEM((pairs * own_rows, columns), bf16),
+            pltpu.VMEM((n_sec, 2, pairs * own_rows, columns), bf16),
             exchange,
             exchange,
             exchange,
             exchange,
-            pltpu.VMEM((own_rows, width), bf16),
+            pltpu.VMEM((2, own_rows, width // 2), bf16),
             pltpu.VMEM((blocks, own_rows, width), bf16),
             pltpu.VMEM((blocks, own_rows, width), bf16),
             pltpu.VMEM((heads, width, 3 * HEAD), bf16),
@@ -491,12 +515,12 @@
             dma((heads, att_pieces)),
             dma((heads, att_pieces)),
             dma,
-            dma((n_sec,)),
-            dma((n_sec,)),
-            dma((n_sec, pairs)),
-            dma((n_sec, pairs)),
-            dma,
-            dma,
+            dma((n_sec, 2)),
+            dma((n_sec, 2)),
+            dma((n_sec, 2, pairs)),
+            dma((n_sec, 2, pairs)),
+            dma((2,)),
+            dma((2,)),
         ],
         compiler_params=pltpu.CompilerParams(
             collective_id=0, has_side_effects=True, vmem_limit_bytes=62 * 1024 * 1024

time: 154 us -> 150 us (0.974)
  Pallas kernels: 152 us -> 148 us
    pallas_call x1, Pallas kernels: 152 us -> 148 us  [on_device(): pl.pallas_call(functools.partial(attend_kernel, n_sec, n_cp, n_tp), out_s...]
where the time goes in v5:
time: 150 us
  Pallas kernels  148 us (99%)
  local copies, waits for them, and re-layouts  1.88 us (1%)
    pallas_call x1, Pallas kernels, on_device(): pl.pallas_call(functools.partial(attend_kernel, n_sec, n_cp, n_tp), out_s...  148 us

profile of v5, /device:TPU:0, one launch (start us, length us, event | category | flops | bytes accessed | tf_op | source)
XLA Modules:
  0.0 150.2 jit_solution(6779385238366058669)
XLA Ops:
  0.0 148.3 %attend.1 = bf16[2,64,2048]{2,1,0:T(8,128)(2,1)} custom-call(bf16[64,2048]{1,0:T(8,128)(2,1)} %rows_ref.1, f32[1,2048]{1,0:T(1,128)} %gain_ref.1, s32[8]{0:T(128)} %owner_ref.1, s32[2]{0:T(128)} %lengths_ref.1, bf16[1,3,2048,2048]{3,2,1,0:T(8,128)(2,1)} %w_ref.1, bf16[1,2048,2048]{2,1,0:T(8,128)(2,1)} %w_out_ref.1), custom_call_target="tpu_custom_call" | custom-call | tf_op jit(solution)/shard_map/attend/pallas_call | solution.py:481
  148.3 1.9 %copy.8 = bf16[2,64,2048]{2,1,0:T(8,128)(2,1)} copy(bf16[2,64,2048]{2,1,0:T(8,128)(2,1)} %attend.1) | data formatting | bytes 1048576

commit v6 on v5

--- a/solution.py
+++ b/solution.py
@@ -209,12 +209,12 @@
             q = (buf[head, at, :HEAD].astype(jnp.float32) * inv_cols[at, :]).astype(jnp.bfloat16)
             scores = lax.dot_general(
                 q, keys[...], (((1,), (1,)), ((), ())), preferred_element_type=jnp.float32
-            ) * (1.0 / math.sqrt(HEAD))
+            )
             spot = pos_k[...]
             allowed = (spot <= pos_q[at, :]) & (spot >= start_q[at, :])
             scores = jnp.where(allowed, scores, -1e30)
             peak = jnp.max(scores, axis=1, keepdims=True)
-            weights = jnp.where(allowed, jnp.exp(scores - peak), 0.0)
+            weights = jnp.exp2((scores - peak) * (math.log2(math.e) / math.sqrt(HEAD)))
             total = jnp.sum(weights, axis=1, keepdims=True)
             mixed = jnp.dot(
                 weights.astype(jnp.bfloat16), values[...], preferred_element_type=jnp.float32
@@ -330,7 +330,7 @@
         return carry
 
     steps = per_way * pieces
-    hop, back_hop, ahead = 3, 4, min(3, lead)
+    hop, back_hop, ahead = 4, 4, min(4, lead)
 
     def decode(i):
         early = i < lead

time: 150 us -> 149 us (level)
  no operation moved by 1% of the time
where the time goes in v6:
time: 149 us
  Pallas kernels  147 us (99%)
  local copies, waits for them, and re-layouts  1.88 us (1%)
    pallas_call x1, Pallas kernels, on_device(): pl.pallas_call(functools.partial(attend_kernel, n_sec, n_cp, n_tp), out_s...  147 us

profile of v6, /device:TPU:0, one launch (start us, length us, event | category | flops | bytes accessed | tf_op | source)
XLA Modules:
  0.0 149.2 jit_solution(9984199536060851014)
XLA Ops:
  0.0 147.3 %attend.1 = bf16[2,64,2048]{2,1,0:T(8,128)(2,1)} custom-call(bf16[64,2048]{1,0:T(8,128)(2,1)} %rows_ref.1, f32[1,2048]{1,0:T(1,128)} %gain_ref.1, s32[8]{0:T(128)} %owner_ref.1, s32[2]{0:T(128)} %lengths_ref.1, bf16[1,3,2048,2048]{3,2,1,0:T(8,128)(2,1)} %w_ref.1, bf16[1,2048,2048]{2,1,0:T(8,128)(2,1)} %w_out_ref.1), custom_call_target="tpu_custom_call" | custom-call | tf_op jit(solution)/shard_map/attend/pallas_call | solution.py:481
  147.3 1.9 %copy.8 = bf16[2,64,2048]{2,1,0:T(8,128)(2,1)} copy(bf16[2,64,2048]{2,1,0:T(8,128)(2,1)} %attend.1) | data formatting | bytes 1048576
